TPU v7x, 256 devices: a whole 4x4x8 slice. The times are simulated.
256 devices in a mesh: region: 32 (over x, z_lo, y), tm: 8 (over z_hi, core).
Axes of the slice: x: 4, y: 4, z: 8 (z_hi: 4, z_lo: 2; z = z_hi * 2 + z_lo), core: 2. Of those that a mesh axis runs over, the one named last changes fastest.
Arguments:
- latents: bfloat16 [32, 1024, 768], P('region', 'tm')
- output_grad: bfloat16 [32, 1024, 768], P('region', 'tm'), may hold values from -6 to 6
- conv_kernel: float32 [4, 768], replicated, may hold values from -1 to 1
- w_query: bfloat16 [768, 768], replicated, may hold values from -0.21875 to 0.21875
- w_key: bfloat16 [768, 768], replicated, may hold values from -0.21875 to 0.21875
- w_value: bfloat16 [768, 768], replicated, may hold values from -0.21875 to 0.21875
- w_out: bfloat16 [768, 768], replicated, may hold values from -0.21875 to 0.21875
- live_counts: int32 [32, 8], P('region', 'tm'), may hold values from 1 to 128, as said below
Outputs:
- input_grad: bfloat16 [32, 1024, 768], P('region', 'tm')
Inputs may be any that keep to these rules, and one draw needn't show every extreme that they name: The first live_counts[r, c] of the 128 tokens of region r in span c are valid.
All inputs are finite; a program needn't handle non-finite values.
Results may differ from a plain program's by a relative error of at most 0.018.
The roundings to bfloat16 on the way count: a program that leaves them out, or rounds other values in their place, can miss the bound.
Values may be sent and summed in bfloat16 or wider, within the bound.
No kernel may reach another device: no remote copies, remote signals or barrier semaphores. Data moves between devices by JAX's collectives and lax.ppermute only.
A program may use at most 128 MiB of HBM per device.

v0:
```python
import math

import jax
import jax.numpy as jnp
from jax import lax
from jax.sharding import PartitionSpec as P

H = 12
KW = 4


def passed_along(block, axis, distance):
    devices = range(lax.axis_size(axis))
    route = [(i - distance, i) for i in devices if i - distance in devices]
    return lax.ppermute(block, axis, route)


def project_back(rows_in, weight):
    return lax.dot_general(
        rows_in, weight, (((1,), (1,)), ((), ())), preferred_element_type=jnp.float32
    )


def largest_divisor(total, limit):
    best = 1
    for option in range(1, min(total, limit) + 1):
        if total % option == 0:
            best = option
    return best


def shards(latents, output_grad, conv_kernel, w_query, w_key, w_value, w_out, live_counts):
    reg_local, span_len, model_width = latents.shape
    head_count = H
    head_dim = model_width // head_count
    row_count = reg_local * span_len
    inv_root = 1.0 / math.sqrt(head_dim)
    edge_rows = passed_along(latents[:, span_len - (KW - 1) :, :], "tm", 1)
    extended = jnp.concatenate([edge_rows, latents], axis=1).astype(jnp.float32)
    convolved = jnp.zeros((reg_local, span_len, model_width), jnp.float32)
    for offset in range(KW):
        convolved = (
            convolved
            + conv_kernel[offset] * extended[:, KW - 1 - offset : KW - 1 - offset + span_len, :]
        )
    hidden = convolved.astype(jnp.bfloat16)
    flattened = hidden.reshape(row_count, model_width)
    queries = jnp.dot(flattened, w_query, preferred_element_type=jnp.float32).astype(jnp.bfloat16)
    position = lax.broadcasted_iota(jnp.int32, (reg_local, span_len), 1)
    query_live = (position < live_counts).astype(jnp.float32).reshape(row_count, 1)
    grad_proj = (
        project_back(output_grad.reshape(row_count, model_width), w_out) * query_live
    ).astype(jnp.bfloat16)
    key_proj = jnp.dot(flattened, w_key, preferred_element_type=jnp.float32).astype(jnp.bfloat16)
    value_proj = jnp.dot(flattened, w_value, preferred_element_type=jnp.float32).astype(
        jnp.bfloat16
    )
    local_pair = jnp.concatenate([key_proj, value_proj], axis=1).reshape(
        reg_local, span_len, 2 * model_width
    )
    pair_all, counts_all = (
        lax.all_gather(local_pair, "region", axis=0, tiled=True),
        lax.all_gather(live_counts, "region", axis=0, tiled=True),
    )
    all_regions = pair_all.shape[0]
    key_live = lax.broadcasted_iota(jnp.int32, (all_regions, span_len), 1) < counts_all
    block_size = min(all_regions, max(1, 1024 // span_len))
    block_total = all_regions // block_size
    query_heads = queries.reshape(row_count, head_count, head_dim)
    grad_heads = grad_proj.reshape(row_count, head_count, head_dim)

    def unpack_block(pair_rows, live_rows):
        key_total = pair_rows.shape[0] * span_len
        flat_pair = pair_rows.reshape(key_total, 2 * model_width)
        key_rows = flat_pair[:, :model_width].reshape(key_total, head_count, head_dim)
        value_rows = flat_pair[:, model_width:].reshape(key_total, head_count, head_dim)
        return (key_rows, value_rows, live_rows.reshape(key_total))

    def scores(key_rows, key_mask):
        logits = (
            jnp.einsum("qhd,khd->hqk", query_heads, key_rows, preferred_element_type=jnp.float32)
            * inv_root
        )
        return jnp.where(key_mask[None, None, :], logits, -1e30)

    block_pairs = pair_all.reshape(block_total, block_size, span_len, 2 * model_width)
    block_lives = key_live.reshape(block_total, block_size, span_len)

    def stat_step(state_pair, block_item):
        running_max, running_sum = state_pair
        key_rows, value_rows, key_mask = unpack_block(block_item[0], block_item[1])
        logits = scores(key_rows, key_mask)
        new_max = jnp.maximum(running_max, jnp.max(logits, axis=2))
        running_sum = running_sum * jnp.exp(running_max - new_max) + jnp.sum(
            jnp.exp(logits - new_max[..., None]), axis=2
        )
        return ((new_max, running_sum), None)

    start_max = jnp.full((head_count, row_count), -1e30, jnp.float32)
    start_sum = jnp.zeros((head_count, row_count), jnp.float32)
    (final_max, final_sum), _ = lax.scan(
        stat_step, (start_max, start_sum), (block_pairs, block_lives)
    )
    log_total = final_max + jnp.log(final_sum)

    def weights_and_grads(key_rows, value_rows, key_mask):
        attention = jnp.exp(scores(key_rows, key_mask) - log_total[..., None])
        weight_grad = jnp.einsum(
            "qhd,khd->hqk", grad_heads, value_rows, preferred_element_type=jnp.float32
        )
        return (attention, weight_grad)

    def delta_step(delta_sum, block_item):
        key_rows, value_rows, key_mask = unpack_block(block_item[0], block_item[1])
        attention, weight_grad = weights_and_grads(key_rows, value_rows, key_mask)
        return (delta_sum + jnp.sum(attention * weight_grad, axis=2), None)

    row_delta, _ = lax.scan(
        delta_step, jnp.zeros((head_count, row_count), jnp.float32), (block_pairs, block_lives)
    )

    def query_step(grad_sum, block_item):
        key_rows, value_rows, key_mask = unpack_block(block_item[0], block_item[1])
        attention, weight_grad = weights_and_grads(key_rows, value_rows, key_mask)
        score_grad = (attention * (weight_grad - row_delta[..., None])).astype(jnp.bfloat16)
        return (
            grad_sum
            + jnp.einsum("hqk,khd->qhd", score_grad, key_rows, preferred_element_type=jnp.float32),
            None,
        )

    query_sum, _ = lax.scan(
        query_step,
        jnp.zeros((row_count, head_count, head_dim), jnp.float32),
        (block_pairs, block_lives),
    )
    query_grad = (query_sum * inv_root).astype(jnp.bfloat16).reshape(row_count, model_width)
    row_total = reg_local * lax.axis_size("region")
    inner = largest_divisor(row_total, block_size)
    pair_rows = pair_all
    live_rows = key_live
    pair_blocks = pair_rows.reshape(row_total // inner, inner, span_len, 2 * model_width)
    live_blocks = live_rows.reshape(row_total // inner, inner, span_len)

    def one_block(block_item):
        key_rows, value_rows, key_mask = unpack_block(block_item[0], block_item[1])
        attention, weight_grad = weights_and_grads(key_rows, value_rows, key_mask)
        score_grad = (attention * (weight_grad - row_delta[..., None])).astype(jnp.bfloat16)
        key_grad = (
            jnp.einsum("hqk,qhd->khd", score_grad, query_heads, preferred_element_type=jnp.float32)
            * inv_root
        )
        value_grad = jnp.einsum(
            "hqk,qhd->khd",
            attention.astype(jnp.bfloat16),
            grad_heads,
            preferred_element_type=jnp.float32,
        )
        key_total = inner * span_len
        both = jnp.concatenate(
            [key_grad.reshape(key_total, model_width), value_grad.reshape(key_total, model_width)],
            axis=1,
        )
        return both.reshape(inner, span_len, 2 * model_width)

    terms = lax.map(one_block, (pair_blocks, live_blocks))
    grad_sums = lax.psum_scatter(
        terms.reshape(row_total, span_len, 2 * model_width).astype(jnp.bfloat16),
        "region",
        scatter_dimension=0,
        tiled=True,
    )
    grad_low = grad_sums.reshape(row_count, 2 * model_width)
    side_grad = project_back(grad_low[:, :model_width], w_key) + project_back(
        grad_low[:, model_width:], w_value
    )
    hidden_grad = project_back(query_grad, w_query) + side_grad
    grad_cube = hidden_grad.reshape(reg_local, span_len, model_width)
    later_rows = passed_along(grad_cube[:, : KW - 1, :], "tm", -1)
    grad_extended = jnp.concatenate([grad_cube, later_rows], axis=1)
    input_grad = jnp.zeros((reg_local, span_len, model_width), jnp.float32)
    for offset in range(KW):
        input_grad = (
            input_grad + conv_kernel[offset] * grad_extended[:, offset : offset + span_len, :]
        )
    return input_grad.astype(jnp.bfloat16)


def solution(mesh):
    in_specs = (
        P("region", "tm", None),
        P("region", "tm", None),
        P(),
        P(),
        P(),
        P(),
        P(),
        P("region", "tm"),
    )
    out_specs = P("region", "tm", None)
    return jax.shard_map(shards, mesh=mesh, in_specs=in_specs, out_specs=out_specs, check_vma=False)
```

profile of v0, /device:TPU:65, one launch (start us, length us, event | category | flops | bytes accessed | tf_op | source)
XLA Modules:
  0.0 652.4 jit_solution(15607879817508255192)
XLA Ops:
  7.3 6.7 %collective-permute-start = (bf16[1,3,768]{2,1,0:T(4,128)(2,1)S(1)}, bf16[1,3,768]{2,1,0:T(4,128)(2,1)S(1)}, u32[]{:S(2)}, u32[]{:S(2)}) collective-permute-start(bf16[1,3,768]{2,1,0:T(4,128)(2,1)S(1)} %slice.71), channel_id=1, source_target_pairs={{0,1},{1,2},{2,3},{3,4},{4,5},{5,6},{6,7},{8,9},{9,10},{10,11},{11... | collective-permute-start | bytes 13832 | tf_op jit(solution)/shard_map/ppermute | solution.py:15
  21.0 14.5 %all-reduce = s32[32]{0:T(128)S(1)} all-reduce(s32[32]{0:T(128)S(1)} %bitcast_dynamic-update-slice_fusion), channel_id=1, replica_groups=mesh['region'=32,'tm'=8] {'region'}, use_global_device_ids=true, to_apply=%add | all-reduce | flops 32 | bytes 256
  38.1 145.0 %all-gather.3.cloned.1.call-done = bf16[4096,1536]{1,0:T(8,128)(2,1)} async-done(((bf16[128,1536]{1,0:T(8,128)(2,1)}), bf16[4096,1536]{1,0:T(8,128)(2,1)}) %all-gather.3.cloned.1.call-update) | async-done | bytes 12582928 | tf_op jit(solution)/shard_map/all_gather | solution.py:62
  183.2 16.7 %copy.22 = bf16[4,8,128,1536]{2,1,3,0:T(8,128)(2,1)} copy(bf16[4,8,128,1536]{3,2,1,0:T(8,128)(2,1)} %bitcast.218) | data formatting | bytes 25165824
  199.9 44.0 %while.46 = (s32[]{:T(128)}, f32[12,128]{1,0:T(8,128)S(1)}, f32[12,128]{1,0:T(8,128)S(1)}, pred[4,8,128]{2,1,0:T(8,128)(4,1)S(1)}, bf16[4,8,128,1536]{2,1,3,0:T(...) while((s32[]{:T(128)}, f32[12,128]{1,0:T(8,128)S(1)}, ...), condition=%wide.region_3.4_spmd.clone, body=%wide.region_0.3_spmd.clone.sunk | while | flops 212344320 | bytes 30165100 | solution.py:101
  243.9 28.2 %while.47 = (s32[]{:T(128)}, f32[12,128]{1,0:T(8,128)S(1)}, pred[4,8,128]{2,1,0:T(8,128)(4,1)S(1)}, bf16[4,8,128,1536]{2,1,3,0:T(8,128)(2,1)}, bf16[128,12,64]{0...) while((s32[]{:T(128)}, f32[12,128]{1,0:T(8,128)S(1)}, ...), condition=%wide.region_6.7_spmd.clone, body=%wide.region_4.6_spmd.clone.sunk | while | flops 410519040 | bytes 35030132 | solution.py:118
  272.2 155.8 %while.45 = (s32[]{:T(128)}, bf16[4,8,128,1536]{3,2,1,0:T(8,128)(2,1)}, pred[4,8,128]{2,1,0:T(8,128)(4,1)S(1)}, bf16[4,8,128,1536]{2,1,3,0:T(8,128)(2,1)}, bf16[...) while((s32[]{:T(128)}, ...), condition=%wide.region_10.11_spmd, body=%wide.region_9.10_spmd.sunk | while | flops 824180736 | bytes 95180944 | solution.py:166
  280.9 7.6 %fusion.119 = bf16[12,1024,64]{1,2,0:T(8,128)(2,1)} fusion(bf16[128,12,64]{0,2,1:T(8,128)(2,1)S(1)} %get-tuple-element.631, f32[12,1024,128]{2,1,0:T(8,128)} %copy-done.1, f32[12,128]{1,0:T(8,128)S(1)} %get-tuple-element.634, f32[12,128]{1,0:T(8,128)S(1)} %get-tuple-element.632, pred[1024]{0:T(1024)(128)(4,1)S(1)} %dynamic-slice_bitcast_fusion.8, ...), kind=kOutput, calls=%fused_computation.13.clone.1 | convolution fusion | flops 413663232 | bytes 9843712 | tf_op jit(solution)/shard_map/while/body/eval_jaxpr/hqk,qhd->khd/dot_general | solution.py:150
  290.4 12.1 %pad_maximum_fusion.4 = bf16[1,8,128,1536]{2,1,3,0:T(8,128)(2,1)} fusion(bf16[1,8,128,768]{2,1,3,0:T(8,128)(2,1)S(1)} %bitcast.206, bf16[1,8,128,768]{2,1,3,0:T(8,128)(2,1)S(1)} %bitcast.207), kind=kLoop, calls=%fused_computation.clone.1 | loop fusion | flops 1572864 | bytes 6291456 | tf_op jit(solution)/shard_map/while/body/eval_jaxpr/concatenate | solution.py:160
  302.5 5.0 copy.62
  319.8 7.6 %fusion.119 = bf16[12,1024,64]{1,2,0:T(8,128)(2,1)} fusion(bf16[128,12,64]{0,2,1:T(8,128)(2,1)S(1)} %get-tuple-element.631, f32[12,1024,128]{2,1,0:T(8,128)} %copy-done.1, f32[12,128]{1,0:T(8,128)S(1)} %get-tuple-element.634, f32[12,128]{1,0:T(8,128)S(1)} %get-tuple-element.632, pred[1024]{0:T(1024)(128)(4,1)S(1)} %dynamic-slice_bitcast_fusion.8, ...), kind=kOutput, calls=%fused_computation.13.clone.1 | convolution fusion | flops 413663232 | bytes 9843712 | tf_op jit(solution)/shard_map/while/body/eval_jaxpr/hqk,qhd->khd/dot_general | solution.py:150
  329.3 12.1 %pad_maximum_fusion.4 = bf16[1,8,128,1536]{2,1,3,0:T(8,128)(2,1)} fusion(bf16[1,8,128,768]{2,1,3,0:T(8,128)(2,1)S(1)} %bitcast.206, bf16[1,8,128,768]{2,1,3,0:T(8,128)(2,1)S(1)} %bitcast.207), kind=kLoop, calls=%fused_computation.clone.1 | loop fusion | flops 1572864 | bytes 6291456 | tf_op jit(solution)/shard_map/while/body/eval_jaxpr/concatenate | solution.py:160
  358.7 7.6 %fusion.119 = bf16[12,1024,64]{1,2,0:T(8,128)(2,1)} fusion(bf16[128,12,64]{0,2,1:T(8,128)(2,1)S(1)} %get-tuple-element.631, f32[12,1024,128]{2,1,0:T(8,128)} %copy-done.1, f32[12,128]{1,0:T(8,128)S(1)} %get-tuple-element.634, f32[12,128]{1,0:T(8,128)S(1)} %get-tuple-element.632, pred[1024]{0:T(1024)(128)(4,1)S(1)} %dynamic-slice_bitcast_fusion.8, ...), kind=kOutput, calls=%fused_computation.13.clone.1 | convolution fusion | flops 413663232 | bytes 9843712 | tf_op jit(solution)/shard_map/while/body/eval_jaxpr/hqk,qhd->khd/dot_general | solution.py:150
  368.2 12.1 %pad_maximum_fusion.4 = bf16[1,8,128,1536]{2,1,3,0:T(8,128)(2,1)} fusion(bf16[1,8,128,768]{2,1,3,0:T(8,128)(2,1)S(1)} %bitcast.206, bf16[1,8,128,768]{2,1,3,0:T(8,128)(2,1)S(1)} %bitcast.207), kind=kLoop, calls=%fused_computation.clone.1 | loop fusion | flops 1572864 | bytes 6291456 | tf_op jit(solution)/shard_map/while/body/eval_jaxpr/concatenate | solution.py:160
  397.6 7.6 %fusion.119 = bf16[12,1024,64]{1,2,0:T(8,128)(2,1)} fusion(bf16[128,12,64]{0,2,1:T(8,128)(2,1)S(1)} %get-tuple-element.631, f32[12,1024,128]{2,1,0:T(8,128)} %copy-done.1, f32[12,128]{1,0:T(8,128)S(1)} %get-tuple-element.634, f32[12,128]{1,0:T(8,128)S(1)} %get-tuple-element.632, pred[1024]{0:T(1024)(128)(4,1)S(1)} %dynamic-slice_bitcast_fusion.8, ...), kind=kOutput, calls=%fused_computation.13.clone.1 | convolution fusion | flops 413663232 | bytes 9843712 | tf_op jit(solution)/shard_map/while/body/eval_jaxpr/hqk,qhd->khd/dot_general | solution.py:150
  407.1 12.1 %pad_maximum_fusion.4 = bf16[1,8,128,1536]{2,1,3,0:T(8,128)(2,1)} fusion(bf16[1,8,128,768]{2,1,3,0:T(8,128)(2,1)S(1)} %bitcast.206, bf16[1,8,128,768]{2,1,3,0:T(8,128)(2,1)S(1)} %bitcast.207), kind=kLoop, calls=%fused_computation.clone.1 | loop fusion | flops 1572864 | bytes 6291456 | tf_op jit(solution)/shard_map/while/body/eval_jaxpr/concatenate | solution.py:160
  419.2 5.0 copy.62
  431.3 54.5 %while.48 = (s32[]{:T(128)}, f32[128,12,64]{0,2,1:T(8,128)}, bf16[4,8,128,1536]{2,1,3,0:T(8,128)(2,1)}, pred[4,8,128]{2,1,0:T(8,128)(4,1)S(1)}, bf16[128,12,64]{...) while((s32[]{:T(128)}, f32[128,12,64]{0,2,1:T(8,128)}, ...), condition=%wide.region_8.9_spmd.clone, body=%wide.region_7.8_spmd.clone.sunk | while | flops 613613568 | bytes 35798140 | solution.py:132
  438.2 6.6 %fusion.137 = f32[128,12,64]{0,2,1:T(8,128)} fusion(bf16[1024,12,64]{0,2,1:T(8,128)(2,1)S(1)} %bitcast.214, f32[12,1024,128]{2,1,0:T(8,128)} %fusion.136, f32[12,128]{1,0:T(8,128)S(1)} %get-tuple-element.663, f32[12,128]{1,0:T(8,128)S(1)} %get-tuple-element.661, pred[1024]{0:T(1024)(128)(4,1)S(1)} %dynamic-slice_bitcast_fusion.11, ...), kind=kOutput, calls=%fused_computation.43.clone.1 | convolution fusion | flops 412286976 | bytes 8860673 | tf_op jit(solution)/shard_map/while/body/eval_jaxpr/hqk,khd->qhd/dot_general | solution.py:128
  451.7 6.8 %fusion.137 = f32[128,12,64]{0,2,1:T(8,128)} fusion(bf16[1024,12,64]{0,2,1:T(8,128)(2,1)S(1)} %bitcast.214, f32[12,1024,128]{2,1,0:T(8,128)} %fusion.136, f32[12,128]{1,0:T(8,128)S(1)} %get-tuple-element.663, f32[12,128]{1,0:T(8,128)S(1)} %get-tuple-element.661, pred[1024]{0:T(1024)(128)(4,1)S(1)} %dynamic-slice_bitcast_fusion.11, ...), kind=kOutput, calls=%fused_computation.43.clone.1 | convolution fusion | flops 412286976 | bytes 8860673 | tf_op jit(solution)/shard_map/while/body/eval_jaxpr/hqk,khd->qhd/dot_general | solution.py:128
  465.5 6.6 %fusion.137 = f32[128,12,64]{0,2,1:T(8,128)} fusion(bf16[1024,12,64]{0,2,1:T(8,128)(2,1)S(1)} %bitcast.214, f32[12,1024,128]{2,1,0:T(8,128)} %fusion.136, f32[12,128]{1,0:T(8,128)S(1)} %get-tuple-element.663, f32[12,128]{1,0:T(8,128)S(1)} %get-tuple-element.661, pred[1024]{0:T(1024)(128)(4,1)S(1)} %dynamic-slice_bitcast_fusion.11, ...), kind=kOutput, calls=%fused_computation.43.clone.1 | convolution fusion | flops 412286976 | bytes 8860673 | tf_op jit(solution)/shard_map/while/body/eval_jaxpr/hqk,khd->qhd/dot_general | solution.py:128
  479.1 6.7 %fusion.137 = f32[128,12,64]{0,2,1:T(8,128)} fusion(bf16[1024,12,64]{0,2,1:T(8,128)(2,1)S(1)} %bitcast.214, f32[12,1024,128]{2,1,0:T(8,128)} %fusion.136, f32[12,128]{1,0:T(8,128)S(1)} %get-tuple-element.663, f32[12,128]{1,0:T(8,128)S(1)} %get-tuple-element.661, pred[1024]{0:T(1024)(128)(4,1)S(1)} %dynamic-slice_bitcast_fusion.11, ...), kind=kOutput, calls=%fused_computation.43.clone.1 | convolution fusion | flops 412286976 | bytes 8860673 | tf_op jit(solution)/shard_map/while/body/eval_jaxpr/hqk,khd->qhd/dot_general | solution.py:128
  487.0 124.6 %reduce-scatter.2.cloned.1.call-done = bf16[1,128,1536]{2,1,0:T(8,128)(2,1)} async-done(((bf16[32,128,1536]{2,1,0:T(8,128)(2,1)}), bf16[1,128,1536]{2,1,0:T(8,128)(2,1)}) %reduce-scatter.2.cloned.1.call-update) | async-done | bytes 393232 | tf_op jit(solution)/shard_map/reduce_scatter | solution.py:167
  615.5 24.8 %collective-permute-start.1 = (f32[1,3,768]{2,1,0:T(4,128)S(1)}, f32[1,3,768]{2,1,0:T(4,128)S(1)}, u32[]{:S(2)}, u32[]{:S(2)}) collective-permute-start(f32[1,3,768]{2,1,0:T(4,128)S(1)} %slice.103), channel_id=1, source_target_pairs={{1,0},{2,1},{3,2},{4,3},{5,4},{6,5},{7,6},{9,8},{10,9},{11,10},{12... | collective-permute-start | bytes 27656 | tf_op jit(solution)/shard_map/ppermute | solution.py:15
  (195 shorter events, 189.0 us)
Async XLA Ops:
  6.5 11.3 %copy-start = (bf16[768,768]{1,0:T(8,128)(2,1)S(1)}, bf16[768,768]{1,0:T(8,128)(2,1)}, u32[]{:S(2)}) copy-start(bf16[768,768]{1,0:T(8,128)(2,1)} %param.20) | copy-start | bytes 3538948
  6.5 176.7 %all-gather.3.cloned.1.call-start = ((), (), s32[]{:S(2)}) async-start(), calls=%async_computation.2 | async-start | bytes 12976128 | tf_op jit(solution)/shard_map/all_gather | solution.py:62
  7.3 7.6 %collective-permute-start = (bf16[1,3,768]{2,1,0:T(4,128)(2,1)S(1)}, bf16[1,3,768]{2,1,0:T(4,128)(2,1)S(1)}, u32[]{:S(2)}, u32[]{:S(2)}) collective-permute-start(bf16[1,3,768]{2,1,0:T(4,128)(2,1)S(1)} %slice.71), channel_id=1, source_target_pairs={{0,1},{1,2},{2,3},{3,4},{4,5},{5,6},{6,7},{8,9},{9,10},{10,11},{11... | collective-permute-start | bytes 13832 | tf_op jit(solution)/shard_map/ppermute | solution.py:15
  14.9 4.1 copy-start.6
  14.9 4.1 copy-start.8
  14.9 4.0 copy-start.10
  14.9 4.0 copy-start.12
  15.9 3.8 copy-start.14
  16.0 19.6 %copy-start.5 = (bf16[1,128,768]{2,1,0:T(8,128)(2,1)S(1)}, bf16[1,128,768]{2,1,0:T(8,128)(2,1)}, u32[]{:S(2)}) copy-start(bf16[1,128,768]{2,1,0:T(8,128)(2,1)} %param.17) | copy-start | bytes 589828
  16.2 21.5 %copy-start.2 = (bf16[768,768]{1,0:T(8,128)(2,1)S(1)}, bf16[768,768]{1,0:T(8,128)(2,1)}, u32[]{:S(2)}) copy-start(bf16[768,768]{1,0:T(8,128)(2,1)} %param.19) | copy-start | bytes 3538948
  19.0 592.6 %reduce-scatter.2.cloned.1.call-start = ((), (), s32[]{:S(2)}) async-start(), calls=%async_computation.1 | async-start | bytes 12976128 | tf_op jit(solution)/shard_map/reduce_scatter | solution.py:167
  277.8 2.7 copy-start.1
  316.7 2.7 copy-start.1
  355.6 2.7 copy-start.1
  394.5 2.7 copy-start.1
  428.0 0.7 copy-start.4
  485.8 129.2 %copy-start.3 = (bf16[768,768]{1,0:T(8,128)(2,1)S(1)}, bf16[768,768]{1,0:T(8,128)(2,1)}, u32[]{:S(2)}) copy-start(bf16[768,768]{1,0:T(8,128)(2,1)} %param.19) | copy-start | bytes 3538948
  486.9 157.7 %copy-start.7 = (f32[768]{0:T(1024)S(1)}, f32[768]{0:T(1024)}, u32[]{:S(2)}) copy-start(f32[768]{0:T(1024)} %copy-done.6) | copy-start | bytes 9220
  487.0 157.7 %copy-start.9 = (f32[768]{0:T(1024)S(1)}, f32[768]{0:T(1024)}, u32[]{:S(2)}) copy-start(f32[768]{0:T(1024)} %copy-done.8) | copy-start | bytes 9220
  487.0 157.7 %copy-start.11 = (f32[768]{0:T(1024)S(1)}, f32[768]{0:T(1024)}, u32[]{:S(2)}) copy-start(f32[768]{0:T(1024)} %copy-done.10) | copy-start | bytes 9220
  487.0 157.7 %copy-start.13 = (f32[768]{0:T(1024)S(1)}, f32[768]{0:T(1024)}, u32[]{:S(2)}) copy-start(f32[768]{0:T(1024)} %copy-done.12) | copy-start | bytes 9220
  615.5 29.1 %collective-permute-start.1 = (f32[1,3,768]{2,1,0:T(4,128)S(1)}, f32[1,3,768]{2,1,0:T(4,128)S(1)}, u32[]{:S(2)}, u32[]{:S(2)}) collective-permute-start(f32[1,3,768]{2,1,0:T(4,128)S(1)} %slice.103), channel_id=1, source_target_pairs={{1,0},{2,1},{3,2},{4,3},{5,4},{6,5},{7,6},{9,8},{10,9},{11,10},{12... | collective-permute-start | bytes 27656 | tf_op jit(solution)/shard_map/ppermute | solution.py:15
Sparse Core Ops, SparseCore 0:
  19.1 164.0 all-gather.2
  428.1 183.4 reduce-scatter.1
where the time goes:
time: 655 us; the launch traced here: 652 us
  waiting for transfers between devices  274 us (42%)
  matrix products  127 us (19%)
  local copies, waits for them, and re-layouts  123 us (19%)
  other arithmetic  67.2 us (10%)
  starting transfers between devices  31.5 us (5%)
  blocking collectives  14.5 us (2%)
  between operations  14.4 us (2%)
    all_gather x1, waiting for transfers between devices, shards(): lax.all_gather(local_pair, 'region', axis=0, tiled=True)  145 us
    reduce_scatter x1, waiting for transfers between devices, shards(): lax.psum_scatter(terms.reshape(row_total, span_len, 2 * model_width).asty...  125 us
    concatenate x4, other arithmetic, one_block(): jnp.concatenate([key_grad.reshape(key_total, model_width), value_grad.res...  48.4 us
    dynamic_update_slice x8, local copies, waits for them, and re-layouts, shards(): terms = lax.map(one_block, (pair_blocks, live_blocks))  35.1 us
    dynamic_slice x16, local copies, waits for them, and re-layouts, shards(): lax.scan(stat_step, (start_max, start_sum), (block_pairs, block_lives))  32.2 us
    ppermute x2, starting transfers between devices, passed_along(): return lax.ppermute(block, axis, route)  31.5 us
    dot_general x4, matrix products, one_block(): jnp.einsum('hqk,qhd->khd', score_grad, query_heads, preferred_element_typ...  30.5 us
    dot_general x4, matrix products, query_step(): jnp.einsum('hqk,khd->qhd', score_grad, key_rows, preferred_element_type=j...  26.7 us
  transfers between devices with their start and end apart: 4, of which 3 were waited for; matrix products, arithmetic and copies ran while one was open for 10% of the time, Pallas kernels for 0%

commit v1 on v0

v1 whole, which is shorter than its diff:
```python
import functools
import math

import jax
import jax.numpy as jnp
from jax import lax
from jax.experimental import pallas as pl
from jax.experimental.pallas import tpu as pltpu
from jax.sharding import PartitionSpec as P

H = 12
HD = 64
KW = 4
WAYS = 2
BLOCK = 16
KEY_STEP = 256
QUERY_STEP = 256
MASKED = -1e30
VMEM_BYTES = 56 * 1024 * 1024
BF16 = jnp.bfloat16
F32 = jnp.float32


def passed_along(block, axis, distance):
    devices = range(lax.axis_size(axis))
    route = [(i - distance, i) for i in devices if i - distance in devices]
    return lax.ppermute(block, axis, route)


def times(left, right):
    return lax.dot_general(left, right, (((1,), (0,)), ((), ())), preferred_element_type=F32)


def times_back(left, right):
    return lax.dot_general(left, right, (((1,), (1,)), ((), ())), preferred_element_type=F32)


def vmem():
    return pl.BlockSpec(memory_space=pltpu.VMEM)


def smem():
    return pl.BlockSpec(memory_space=pltpu.SMEM)


def params():
    return pltpu.CompilerParams(vmem_limit_bytes=VMEM_BYTES)


def project_kernel(
    place_ref, latents_ref, edge_ref, grad_ref, taps_ref, wq_ref, wk_ref, wv_ref, wo_ref, send_ref, qg_ref
):
    span = latents_ref.shape[0]
    region, live = place_ref[0], place_ref[1]
    extended = jnp.concatenate([edge_ref[...].astype(F32), latents_ref[...].astype(F32)], axis=0)
    convolved = jnp.zeros(latents_ref.shape, F32)
    for offset in range(KW):
        start = KW - 1 - offset
        convolved = convolved + taps_ref[offset : offset + 1, :] * extended[start : start + span, :]
    hidden = convolved.astype(BF16)
    rows = lax.broadcasted_iota(jnp.int32, (span, 1), 0)
    alive = (rows < live).astype(F32)
    grads = (times_back(grad_ref[...], wo_ref[...]) * alive).astype(BF16)
    queries = (times(hidden, wq_ref[...]).astype(BF16).astype(F32) * (1.0 / math.sqrt(HD))).astype(BF16)
    keys = times(hidden, wk_ref[...]).astype(BF16)
    values = times(hidden, wv_ref[...]).astype(BF16)
    count = jnp.zeros((BLOCK, 2 * HD), F32) + live.astype(F32)
    count = count.astype(BF16)
    for head in range(H):
        cut = slice(head * HD, (head + 1) * HD)
        pair = jnp.concatenate([keys[:, cut], values[:, cut]], axis=1)
        qg_ref[...] = jnp.concatenate([queries[:, cut], grads[:, cut]], axis=1)
        for half in range(WAYS):
            send_ref[head * WAYS + half, :span, :] = pair
            send_ref[head * WAYS + half, span + span // WAYS :, :] = count
        for block in range(span // BLOCK):
            half = lax.rem(block + region, WAYS)
            to = span + (block // WAYS) * BLOCK
            send_ref[head * WAYS + half, to : to + BLOCK, :] = qg_ref[block * BLOCK : (block + 1) * BLOCK, :]


def attend_kernel(
    place_ref,
    recv_ref,
    send_ref,
    kaug_ref,
    kv_ref,
    kt_ref,
    qg_ref,
    qa_ref,
    gm_ref,
    p_ref,
    wg_ref,
    top_ref,
    dkv_ref,
    dq_ref,
    koff_ref,
    qoff_ref,
):
    regions = recv_ref.shape[0]
    span = kv_ref.shape[0] // regions
    share = span // WAYS
    me = place_ref[0]
    half = lax.rem(me, WAYS)
    busy = me < H * WAYS
    lane_k = lax.broadcasted_iota(jnp.int32, (span, 2 * HD), 1)
    row_k = lax.broadcasted_iota(jnp.int32, (span, 2 * HD), 0)
    lane_q = lax.broadcasted_iota(jnp.int32, (share, 2 * HD), 1)

    @pl.when(busy)
    def _():
        lane = lax.broadcasted_iota(jnp.int32, (KEY_STEP, 2 * HD), 1)
        blank = jnp.where(lane == HD, MASKED, 0.0).astype(BF16)
        none = jnp.zeros((KEY_STEP, 2 * HD), BF16)
        for step in range(kaug_ref.shape[0] // KEY_STEP):
            kaug_ref[step * KEY_STEP : (step + 1) * KEY_STEP, :] = blank
            kv_ref[step * KEY_STEP : (step + 1) * KEY_STEP, :] = none
            dkv_ref[step * KEY_STEP : (step + 1) * KEY_STEP, :] = jnp.zeros((KEY_STEP, 2 * HD), F32)
        for step in range(qg_ref.shape[0] // QUERY_STEP):
            qg_ref[step * QUERY_STEP : (step + 1) * QUERY_STEP, :] = none
            qa_ref[step * QUERY_STEP : (step + 1) * QUERY_STEP, :] = none
            gm_ref[step * QUERY_STEP : (step + 1) * QUERY_STEP, :] = none

    def compact(region, totals):
        key_at, query_at = totals
        koff_ref[region] = key_at
        qoff_ref[region] = query_at
        live = jnp.max(recv_ref[region, span + share :, :].astype(F32)).astype(jnp.int32)
        live = jnp.where(busy, jnp.clip(live, 0, span), 0)
        blocks = lax.div(live + BLOCK - 1, BLOCK)
        pair = recv_ref[region, :span, :].astype(F32)
        kv_ref[pl.ds(pl.multiple_of(key_at, BLOCK), span), :] = pair.astype(BF16)
        bias = jnp.where(row_k < live, 0.0, MASKED)
        kaug = jnp.where(lane_k < HD, pair, jnp.where(lane_k == HD, bias, 0.0))
        kaug_ref[pl.ds(pl.multiple_of(key_at, BLOCK), span), :] = kaug.astype(BF16)
        both = recv_ref[region, span : span + share, :].astype(F32)
        to = pl.ds(pl.multiple_of(query_at, BLOCK), share)
        qg_ref[to, :] = both.astype(BF16)
        qa_ref[to, :] = jnp.where(lane_q < HD, both, jnp.where(lane_q == HD, 1.0, 0.0)).astype(BF16)
        gm_ref[to, :] = jnp.where(lane_q >= HD, both, 0.0).astype(BF16)
        mine = lax.div(blocks + 1 - lax.rem(half + region, WAYS), WAYS)
        return (key_at + blocks * BLOCK, query_at + mine * BLOCK)

    zero = jnp.int32(0)
    key_total, query_total = lax.fori_loop(0, regions, compact, (zero, zero))
    key_steps = lax.div(key_total + KEY_STEP - 1, KEY_STEP)
    query_steps = lax.div(query_total + QUERY_STEP - 1, QUERY_STEP)

    def turn(step, carry):
        keys = kaug_ref[pl.ds(pl.multiple_of(step * KEY_STEP, KEY_STEP), KEY_STEP), :]
        kt_ref[step] = keys.astype(F32).T[:HD, :].astype(BF16)
        return carry

    lax.fori_loop(0, key_steps, turn, 0)

    def query_block(block, carry):
        at = pl.ds(pl.multiple_of(block * QUERY_STEP, QUERY_STEP), QUERY_STEP)

        def gather(step, state):
            top, total, dot = state
            here = pl.ds(pl.multiple_of(step * KEY_STEP, KEY_STEP), KEY_STEP)
            logits = times_back(kaug_ref[here, :], qa_ref[at, :]).reshape(KEY_STEP // 8, 8, QUERY_STEP)
            weight_grad = times_back(kv_ref[here, :], gm_ref[at, :]).reshape(KEY_STEP // 8, 8, QUERY_STEP)
            new_top = jnp.maximum(top, jnp.max(logits, axis=0))
            shrink = jnp.exp(top - new_top)
            raised = jnp.exp(logits - new_top[None])
            p_ref[step] = raised
            wg_ref[step] = weight_grad
            top_ref[step] = new_top
            total = total * shrink + jnp.sum(raised, axis=0)
            dot = dot * shrink + jnp.sum(raised * weight_grad, axis=0)
            return (new_top, total, dot)

        none = jnp.zeros((8, QUERY_STEP), F32)
        top, total, dot = lax.fori_loop(0, key_steps, gather, (none + MASKED, none, none))
        best = jnp.max(top, axis=0, keepdims=True)
        shrink = jnp.exp(top - best)
        whole = jnp.sum(total * shrink, axis=0, keepdims=True)
        inverse = 1.0 / whole
        delta = jnp.sum(dot * shrink, axis=0, keepdims=True) * inverse

        def spread(step, query_grad):
            here = pl.ds(pl.multiple_of(step * KEY_STEP, KEY_STEP), KEY_STEP)
            factor = jnp.exp(top_ref[step] - best) * inverse
            attention = p_ref[step] * factor[None]
            score_grad = attention * (wg_ref[step] - delta[None])
            attention = attention.reshape(KEY_STEP, QUERY_STEP).astype(BF16)
            score_grad = score_grad.reshape(KEY_STEP, QUERY_STEP).astype(BF16)
            both = qg_ref[at, :]
            lane = lax.broadcasted_iota(jnp.int32, (KEY_STEP, 2 * HD), 1)
            dkv_ref[here, :] += jnp.where(lane < HD, times(score_grad, both), times(attention, both))
            return query_grad + times(kt_ref[step], score_grad)

        query_grad = lax.fori_loop(0, key_steps, spread, jnp.zeros((HD, QUERY_STEP), F32))
        query_grad = query_grad * (1.0 / math.sqrt(HD))
        dq_ref[at, :] = jnp.concatenate([query_grad, query_grad], axis=0).T
        return carry

    lax.fori_loop(0, query_steps, query_block, 0)

    def give_back(region, carry):
        here = pl.ds(pl.multiple_of(koff_ref[region], BLOCK), span)
        send_ref[region, :span, :] = dkv_ref[here, :].astype(BF16)
        first = dq_ref[pl.ds(pl.multiple_of(qoff_ref[region], BLOCK), share // 2), :]
        second = dq_ref[pl.ds(pl.multiple_of(qoff_ref[region] + share // 2, BLOCK), share // 2), :]
        lane = lax.broadcasted_iota(jnp.int32, (share // 2, 2 * HD), 1)
        send_ref[region, span:, :] = jnp.where(lane < HD, first, second).astype(BF16)
        return carry

    lax.fori_loop(0, regions, give_back, 0)


def return_kernel(place_ref, recv_ref, wq_ref, wk_ref, wv_ref, hidden_grad_ref, dk_ref, dv_ref, dq_ref):
    span = hidden_grad_ref.shape[0]
    quarter = span // WAYS // 2
    region, live = place_ref[0], place_ref[1]
    alive = lax.broadcasted_iota(jnp.int32, (span, 1), 0) < live
    for duo in range(H // 2):
        cut = slice(duo * 2 * HD, (duo + 1) * 2 * HD)
        left, right = 2 * duo * WAYS, (2 * duo + 1) * WAYS
        first = recv_ref[left, :span, :].astype(F32) + recv_ref[left + 1, :span, :].astype(F32)
        second = recv_ref[right, :span, :].astype(F32) + recv_ref[right + 1, :span, :].astype(F32)
        key_grad = jnp.concatenate([first[:, :HD], second[:, :HD]], axis=1)
        value_grad = jnp.concatenate([first[:, HD:], second[:, HD:]], axis=1)
        dk_ref[:, cut] = jnp.where(alive, key_grad, 0.0).astype(BF16)
        dv_ref[:, cut] = jnp.where(alive, value_grad, 0.0).astype(BF16)
        for half in range(WAYS):
            shift = lax.rem(half + region, WAYS)
            one = recv_ref[left + half, span:, :].astype(F32)
            two = recv_ref[right + half, span:, :].astype(F32)
            low = jnp.concatenate([one[:, :HD], two[:, :HD]], axis=1)
            high = jnp.concatenate([one[:, HD:], two[:, HD:]], axis=1)
            for number, part in enumerate((low, high)):
                for piece in range(quarter // BLOCK):
                    index = number * (quarter // BLOCK) + piece
                    to = pl.multiple_of((WAYS * index + shift) * BLOCK, BLOCK)
                    dq_ref[pl.ds(to, BLOCK), cut] = part[piece * BLOCK : (piece + 1) * BLOCK, :]
    query_grad = jnp.where(alive, dq_ref[...], 0.0).astype(BF16)
    hidden_grad_ref[...] = times_back(query_grad, wq_ref[...]) + (
        times_back(dk_ref[...], wk_ref[...]) + times_back(dv_ref[...], wv_ref[...])
    )


def shards(latents, output_grad, conv_kernel, w_query, w_key, w_value, w_out, live_counts):
    _, span, width = latents.shape
    regions = lax.axis_size("region")
    share = span // WAYS
    region = lax.axis_index("region").astype(jnp.int32)
    place = jnp.stack([region, live_counts[0, 0]])
    edge = passed_along(latents[:, span - (KW - 1) :, :], "tm", 1)
    sent = pl.pallas_call(
        project_kernel,
        name="project",
        out_shape=jax.ShapeDtypeStruct((regions, span + share + BLOCK, 2 * HD), BF16),
        in_specs=[smem()] + [vmem()] * 8,
        out_specs=vmem(),
        scratch_shapes=[pltpu.VMEM((span, 2 * HD), BF16)],
        compiler_params=params(),
    )(place, latents[0], edge[0], output_grad[0], conv_kernel, w_query, w_key, w_value, w_out)
    gathered = lax.all_to_all(sent, "region", 0, 0, tiled=True)
    keys, queries = regions * span, regions * share
    key_steps = keys // KEY_STEP
    grads = pl.pallas_call(
        attend_kernel,
        name="attend",
        out_shape=jax.ShapeDtypeStruct((regions, span + share // 2, 2 * HD), BF16),
        in_specs=[smem(), vmem()],
        out_specs=vmem(),
        scratch_shapes=[
            pltpu.VMEM((keys, 2 * HD), BF16),
            pltpu.VMEM((keys, 2 * HD), BF16),
            pltpu.VMEM((key_steps, HD, KEY_STEP), BF16),
            pltpu.VMEM((queries, 2 * HD), BF16),
            pltpu.VMEM((queries, 2 * HD), BF16),
            pltpu.VMEM((queries, 2 * HD), BF16),
            pltpu.VMEM((key_steps, KEY_STEP // 8, 8, QUERY_STEP), F32),
            pltpu.VMEM((key_steps, KEY_STEP // 8, 8, QUERY_STEP), F32),
            pltpu.VMEM((key_steps, 8, QUERY_STEP), F32),
            pltpu.VMEM((keys, 2 * HD), F32),
            pltpu.VMEM((queries, 2 * HD), F32),
            pltpu.SMEM((regions,), jnp.int32),
            pltpu.SMEM((regions,), jnp.int32),
        ],
        compiler_params=params(),
    )(place, gathered)
    returned = lax.all_to_all(grads, "region", 0, 0, tiled=True)
    hidden_grad = pl.pallas_call(
        return_kernel,
        name="project_back",
        out_shape=jax.ShapeDtypeStruct((span, width), F32),
        in_specs=[smem()] + [vmem()] * 4,
        out_specs=vmem(),
        scratch_shapes=[
            pltpu.VMEM((span, width), BF16),
            pltpu.VMEM((span, width), BF16),
            pltpu.VMEM((span, width), F32),
        ],
        compiler_params=params(),
    )(place, returned, w_query, w_key, w_value)
    grad_cube = hidden_grad[None]
    later_rows = passed_along(grad_cube[:, : KW - 1, :], "tm", -1)
    grad_extended = jnp.concatenate([grad_cube, later_rows], axis=1)
    input_grad = jnp.zeros((1, span, width), F32)
    for offset in range(KW):
        input_grad = input_grad + conv_kernel[offset] * grad_extended[:, offset : offset + span, :]
    return input_grad.astype(BF16)


def solution(mesh):
    in_specs = (
        P("region", "tm", None),
        P("region", "tm", None),
        P(),
        P(),
        P(),
        P(),
        P(),
        P("region", "tm"),
    )
    out_specs = P("region", "tm", None)
    return jax.shard_map(shards, mesh=mesh, in_specs=in_specs, out_specs=out_specs, check_vma=False)
```

time: 655 us -> 112 us (0.17)
  waiting for transfers between devices: 274 us -> 5.14 us
  matrix products: 127 us -> 0 us
  local copies, waits for them, and re-layouts: 123 us -> 2.08 us
  other arithmetic: 67.2 us -> 2.98 us
  Pallas kernels: 0 us -> 42.7 us
  blocking collectives: 14.5 us -> 50.1 us
  starting transfers between devices: 31.5 us -> 8.57 us
  between operations: 14.4 us -> 0.69 us
    all_gather x1 -> x0, waiting for transfers between devices: 145 us -> none  [shards(): lax.all_gather(local_pair, 'region', axis=0, tiled=True)]
    dot_general x39 -> x0, matrix products: 127 us -> none  [the longest x4 30.5 us: one_block(): jnp.einsum('hqk,qhd->khd', score_grad, query_heads, preferred_element_typ...]
    reduce_scatter x1 -> x0, waiting for transfers between devices: 125 us -> none  [shards(): lax.psum_scatter(terms.reshape(row_total, span_len, 2 * model_width).asty...]
    all_to_all x0 -> x2, blocking collectives: none -> 50.1 us  [the longest x1 31.9 us: shards(): gathered = lax.all_to_all(sent, 'region', 0, 0, tiled=True)]
    concatenate x5 -> x0, other arithmetic: 49.2 us -> none  [the longest x4 48.4 us: one_block(): jnp.concatenate([key_grad.reshape(key_total, model_width), value_grad.res...]
    pallas_call x0 -> x3, Pallas kernels: none -> 42.7 us  [the longest x1 33.2 us: shards(): pl.pallas_call(attend_kernel, name='attend', out_shape=jax.ShapeDtypeStru...]
    dynamic_update_slice x8 -> x0, local copies, waits for them, and re-layouts: 35.1 us -> none  [shards(): terms = lax.map(one_block, (pair_blocks, live_blocks))]
    dynamic_slice x16 -> x0, local copies, waits for them, and re-layouts: 32.2 us -> none  [shards(): lax.scan(stat_step, (start_max, start_sum), (block_pairs, block_lives))]
  transfers between devices with their start and end apart: 4 -> 2, of which waited for: 3 -> 1; matrix products, arithmetic and copies ran while one was open for 10% -> 1% of each run, Pallas kernels for 0% -> 0%
where the time goes in v1:
time: 112 us
  blocking collectives  50.1 us (45%)
  Pallas kernels  42.7 us (38%)
  starting transfers between devices  8.57 us (8%)
  waiting for transfers between devices  5.14 us (5%)
  other arithmetic  2.98 us (3%)
  local copies, waits for them, and re-layouts  2.08 us (2%)
    pallas_call x1, Pallas kernels, shards(): pl.pallas_call(attend_kernel, name='attend', out_shape=jax.ShapeDtypeStru...  33.2 us
    all_to_all x1, blocking collectives, shards(): gathered = lax.all_to_all(sent, 'region', 0, 0, tiled=True)  31.9 us
    all_to_all x1, blocking collectives, shards(): returned = lax.all_to_all(grads, 'region', 0, 0, tiled=True)  18.3 us
    ppermute x2, starting transfers between devices, passed_along(): return lax.ppermute(block, axis, route)  8.57 us
    ppermute x2, waiting for transfers between devices, passed_along(): return lax.ppermute(block, axis, route)  5.14 us
    pallas_call x1, Pallas kernels, shards(): pl.pallas_call(project_kernel, name='project', out_shape=jax.ShapeDtypeSt...  4.95 us
    pallas_call x1, Pallas kernels, shards(): pl.pallas_call(return_kernel, name='project_back', out_shape=jax.ShapeDty...  4.47 us
    convert_element_type x1, other arithmetic, shards(): return input_grad.astype(BF16)  2.39 us
  transfers between devices with their start and end apart: 2, of which 1 were waited for; matrix products, arithmetic and copies ran while one was open for 1% of the time, Pallas kernels for 0%

profile of v1, /device:TPU:65, one launch (start us, length us, event | category | flops | bytes accessed | tf_op | source)
XLA Modules:
  0.0 112.3 jit_solution(18074695050258299221)
XLA Ops:
  0.0 0.7 slice.28
  0.7 6.7 %collective-permute-start = (bf16[1,3,768]{2,1,0:T(4,128)(2,1)S(1)}, bf16[1,3,768]{2,1,0:T(4,128)(2,1)S(1)}, u32[]{:S(2)}, u32[]{:S(2)}) collective-permute-start(bf16[1,3,768]{2,1,0:T(4,128)(2,1)S(1)} %slice.28), channel_id=1, source_target_pairs={{0,1},{1,2},{2,3},{3,4},{4,5},{5,6},{6,7},{8,9},{9,10},{10,11},{11... | collective-permute-start | bytes 13832 | tf_op jit(solution)/shard_map/ppermute | solution.py:27
  8.0 0.6 pad_add_fusion.place_ref
  8.6 0.0 collective-permute-done
  8.6 0.0 copy-start.1
  8.6 0.6 copy-done.1
  9.2 4.9 %project.1 = bf16[32,208,128]{2,1,0:T(8,128)(2,1)} custom-call(s32[2]{0:T(128)} %pad_add_fusion.place_ref, bf16[128,768]{1,0:T(8,128)(2,1)} %bitcast.11, bf16[3,768]{1,0:T(4,128)(2,1)} %bitcast.13, bf16[128,768]{1,0:T(8,128)(2,1)} %bitcast.12, f32[4,768]{1,0:T(4,128)} %taps_ref.1, bf16[768,768]{1,0:T(8,128)(2,1)} %wq_ref.3, bf16[768,768]{1,0:T(8,128)(2,1)} %wk_ref.3, ...), custom_call_target="tpu_custom_call" | custom-call | tf_op jit(solution)/shard_map/project/pallas_call | solution.py:251
  14.2 31.9 %all_to_all.10.recv_ref = bf16[32,208,128]{2,1,0:T(8,128)(2,1)} all-to-all(bf16[32,208,128]{2,1,0:T(8,128)(2,1)} %project.1), channel_id=1, replica_groups=mesh['region'=32,'tm'=8] {'region'}, dimensions={0} | all-to-all | bytes 3407872 | tf_op jit(solution)/shard_map/all_to_all | solution.py:260
  46.0 33.2 %attend.1 = bf16[32,160,128]{2,1,0:T(8,128)(2,1)} custom-call(s32[2]{0:T(128)} %pad_add_fusion.place_ref, bf16[32,208,128]{2,1,0:T(8,128)(2,1)} %all_to_all.10.recv_ref), custom_call_target="tpu_custom_call" | custom-call | tf_op jit(solution)/shard_map/attend/pallas_call | solution.py:263
  79.3 18.3 %all_to_all.11.recv_ref = bf16[32,160,128]{2,1,0:T(8,128)(2,1)} all-to-all(bf16[32,160,128]{2,1,0:T(8,128)(2,1)} %attend.1), channel_id=1, replica_groups=mesh['region'=32,'tm'=8] {'region'}, dimensions={0} | all-to-all | bytes 2621440 | tf_op jit(solution)/shard_map/all_to_all | solution.py:286
  97.5 0.0 copy-start
  97.6 4.5 %project_back.1 = f32[128,768]{1,0:T(8,128)} custom-call(s32[2]{0:T(128)} %pad_add_fusion.place_ref, bf16[32,160,128]{2,1,0:T(8,128)(2,1)} %all_to_all.11.recv_ref, bf16[768,768]{1,0:T(8,128)(2,1)} %wq_ref.3, bf16[768,768]{1,0:T(8,128)(2,1)} %wk_ref.3, bf16[768,768]{1,0:T(8,128)(2,1)} %wv_ref.3), custom_call_target="tpu_custom_call" | custom-call | tf_op jit(solution)/shard_map/project_back/pallas_call | solution.py:287
  102.0 0.7 slice.36
  102.8 1.9 %collective-permute-start.1 = (f32[1,3,768]{2,1,0:T(4,128)S(1)}, f32[1,3,768]{2,1,0:T(4,128)S(1)}, u32[]{:S(2)}, u32[]{:S(2)}) collective-permute-start(f32[1,3,768]{2,1,0:T(4,128)S(1)} %slice.36), channel_id=1, source_target_pairs={{1,0},{2,1},{3,2},{4,3},{5,4},{6,5},{7,6},{9,8},{10,9},{11,10},{12... | collective-permute-start | bytes 27656 | tf_op jit(solution)/shard_map/ppermute | solution.py:27
  104.7 0.0 copy-done
  104.7 5.1 %collective-permute-done.1 = f32[1,3,768]{2,1,0:T(4,128)S(1)} collective-permute-done((f32[1,3,768]{2,1,0:T(4,128)S(1)}, f32[1,3,768]{2,1,0:T(4,128)S(1)}, u32[]{:S(2)}, u32[]{:S(2)}) %collective-permute-start.1) | collective-permute-done | bytes 9248 | tf_op jit(solution)/shard_map/ppermute | solution.py:27
  109.9 2.4 %fusion.4 = bf16[1,128,768]{2,1,0:T(8,128)(2,1)} fusion(f32[1,128,768]{2,1,0:T(8,128)} %bitcast.10, f32[1,3,768]{2,1,0:T(4,128)S(1)} %collective-permute-done.1, f32[128,768]{1,0:T(8,128)} %project_back.1, f32[768]{0:T(1024)S(1)} %get-tuple-element.7, f32[768]{0:T(1024)S(1)} %get-tuple-element.8, f32[768]{0:T(1024)S(1)} %get-tuple-element.6, ...), kind=kLoop, calls=%fused_computation.8 | loop fusion | flops 1081344 | bytes 1004544 | tf_op jit(solution)/shard_map/convert_element_type | solution.py:306
  (1 shorter events, 0.0 us)
Async XLA Ops:
  0.7 7.9 %collective-permute-start = (bf16[1,3,768]{2,1,0:T(4,128)(2,1)S(1)}, bf16[1,3,768]{2,1,0:T(4,128)(2,1)S(1)}, u32[]{:S(2)}, u32[]{:S(2)}) collective-permute-start(bf16[1,3,768]{2,1,0:T(4,128)(2,1)S(1)} %slice.28), channel_id=1, source_target_pairs={{0,1},{1,2},{2,3},{3,4},{4,5},{5,6},{6,7},{8,9},{9,10},{10,11},{11... | collective-permute-start | bytes 13832 | tf_op jit(solution)/shard_map/ppermute | solution.py:27
  8.6 0.6 copy-start.1
  97.5 7.1 %copy-start = (f32[4,768]{1,0:T(4,128)S(1)}, f32[4,768]{1,0:T(4,128)}, u32[]{:S(2)}) copy-start(f32[4,768]{1,0:T(4,128)} %taps_ref.1) | copy-start | bytes 36868
  102.8 7.1 %collective-permute-start.1 = (f32[1,3,768]{2,1,0:T(4,128)S(1)}, f32[1,3,768]{2,1,0:T(4,128)S(1)}, u32[]{:S(2)}, u32[]{:S(2)}) collective-permute-start(f32[1,3,768]{2,1,0:T(4,128)S(1)} %slice.36), channel_id=1, source_target_pairs={{1,0},{2,1},{3,2},{4,3},{5,4},{6,5},{7,6},{9,8},{10,9},{11,10},{12... | collective-permute-start | bytes 27656 | tf_op jit(solution)/shard_map/ppermute | solution.py:27
